TPU v7x, 32 devices: a whole 2x2x4 slice. The times are simulated.
32 devices in a mesh: req: 8 (over y, x, core), tp: 4 (over z).
Axes of the slice: x: 2, y: 2, z: 4, core: 2. Of those that a mesh axis runs over, the one named last changes fastest.
Arguments:
- tokens: bfloat16 [2048, 2560], P('req'), may hold values from -6 to 6
- norm_gain: float32 [2560], replicated, may hold values from 0.1 to 1.9
- w_query: bfloat16 [2560, 2560], P(None, 'tp')
- w_key: bfloat16 [2560, 640], P(None, 'tp')
- w_value: bfloat16 [2560, 640], P(None, 'tp'), may hold values from -0.125 to 0.125
- page_counts: int32 [4], replicated, may hold values from 1 to 64, 128 in all
- pad_counts: int32 [4], replicated, may hold values from 0 to 15
- page_table: int32 [8, 16], P('req'), may hold values from 0 to 15, each once within a row
Outputs:
- context: bfloat16 [2048, 2560], P('req', 'tp')
- cache: bfloat16 [128, 8, 2560], P(('req', 'tp'))
Inputs may be any that keep to these rules, and one draw needn't show every extreme that they name: `page_counts`: each prompt has at least one live slot; the slots of all prompts fill the stream exactly. `page_table`: each row is a permutation; cache slot s of a block belongs to tp index s // 4.
All inputs are finite; a program needn't handle non-finite values.
Results may differ from a plain program's by a relative error of at most 0.012.
Values may be sent and summed in bfloat16 or wider, within the bound.
A program may use at most 64 MiB of HBM per device.

v0:
```python
import jax
import jax.numpy as jnp
from jax import lax
from jax.sharding import PartitionSpec as P

HD = 80
WINDOW = 4096
PAGE = 16


NORM_EPS = 1e-05
ROPE_BASE = 10000.0
MASKED_SCORE = -1e30


def passed_along(x, axis, by):
    size = lax.axis_size(axis)
    pairs = [(i, i + by) for i in range(size) if 0 <= i + by < size]
    return lax.ppermute(x, axis, pairs)


def token_meta(slot_index, page_counts, pad_counts):
    prompt_count = page_counts.shape[0]
    slot_counts = page_counts * PAGE
    slot_ends = jnp.cumsum(slot_counts)
    segment_id = jnp.sum((slot_index[:, None] >= slot_ends[None, :]).astype(jnp.int32), axis=1)
    one_hot = (segment_id[:, None] == jnp.arange(prompt_count, dtype=jnp.int32)[None, :]).astype(
        jnp.int32
    )
    first_slot = jnp.sum(one_hot * (slot_ends - slot_counts)[None, :], axis=1)
    live_count = jnp.sum(one_hot * (slot_counts - pad_counts)[None, :], axis=1)
    position = slot_index - first_slot
    inside = slot_index >= 0
    is_live = (position < live_count) & inside
    segment_id = jnp.where(inside, segment_id, -1)
    return (segment_id, position, is_live)


def rotate(vectors, position):
    half_width = vectors.shape[-1] // 2
    frequency = ROPE_BASE ** (-2.0 * jnp.arange(half_width, dtype=jnp.float32) / vectors.shape[-1])
    angles = position.astype(jnp.float32)[:, None, None] * frequency[None, None, :]
    cosine = jnp.cos(angles)
    sine_part = jnp.sin(angles)
    front_half = vectors[..., :half_width]
    back_half = vectors[..., half_width:]
    return jnp.concatenate(
        [front_half * cosine - back_half * sine_part, back_half * cosine + front_half * sine_part],
        axis=-1,
    )


def project(tokens, norm_gain, w_query, w_key, w_value, position):
    row_count = tokens.shape[0]
    as_float = tokens.astype(jnp.float32)
    normed = (
        as_float
        * lax.rsqrt(jnp.mean(as_float * as_float, axis=-1, keepdims=True) + NORM_EPS)
        * norm_gain
    ).astype(jnp.bfloat16)
    query_rot = jnp.dot(normed, w_query, preferred_element_type=jnp.float32).reshape(
        row_count, -1, HD
    )
    query_rot = rotate(query_rot, position).astype(jnp.bfloat16)
    key_rot = jnp.dot(normed, w_key, preferred_element_type=jnp.float32).reshape(row_count, -1, HD)
    key_rot = rotate(key_rot, position).astype(jnp.bfloat16)
    value_rows = (
        jnp.dot(normed, w_value, preferred_element_type=jnp.float32)
        .reshape(row_count, -1, HD)
        .astype(jnp.bfloat16)
    )
    return (query_rot, key_rot, value_rows)


def per_device(tokens, norm_gain, w_query, w_key, w_value, page_counts, pad_counts, page_table):
    row_count = tokens.shape[0]
    stream_total = row_count * lax.axis_size("req")
    longest_prompt = min(8 * row_count, stream_total // 2)
    reach_blocks = min(WINDOW, longest_prompt) // row_count
    block_start = lax.axis_index("req") * row_count
    slot_index = block_start + jnp.arange(row_count, dtype=jnp.int32)
    segment_id, position, is_live = token_meta(slot_index, page_counts, pad_counts)
    query_rot, key_rot, value_rows = project(tokens, norm_gain, w_query, w_key, w_value, position)
    kv_heads = key_rot.shape[1]
    group_size = query_rot.shape[1] // kv_heads
    head_total = kv_heads * group_size
    packed = jnp.concatenate([key_rot, value_rows], axis=-1)
    earlier_blocks = [
        passed_along(packed, "req", reach_blocks - step_id) for step_id in range(reach_blocks)
    ]
    key_blocks = jnp.stack(earlier_blocks + [packed])
    key_index = (
        block_start
        - reach_blocks * row_count
        + jnp.arange((reach_blocks + 1) * row_count, dtype=jnp.int32)
    )
    key_segment, unused_position, key_live = token_meta(key_index, page_counts, pad_counts)
    key_index = key_index.reshape(reach_blocks + 1, row_count)
    key_segment = key_segment.reshape(reach_blocks + 1, row_count)
    key_live = key_live.reshape(reach_blocks + 1, row_count)
    allowed = (key_segment[:, None, :] == segment_id[None, :, None]) & key_live[:, None, :]
    allowed = (
        allowed
        & (key_index[:, None, :] <= slot_index[None, :, None])
        & (slot_index[None, :, None] - key_index[:, None, :] < WINDOW)
    )
    score_scale = HD ** (-0.5)

    def one_head(head_id):
        kv_id = head_id // group_size
        head_queries = lax.dynamic_index_in_dim(query_rot, head_id, 1, keepdims=False)
        head_kv = lax.dynamic_index_in_dim(key_blocks, kv_id, 2, keepdims=False)

        def score_tile(inputs):
            kv_block, block_allowed, block_segment = inputs
            tile = (
                lax.dot_general(
                    head_queries,
                    kv_block[:, :HD],
                    (((1,), (1,)), ((), ())),
                    preferred_element_type=jnp.float32,
                )
                * score_scale
            )
            return jnp.where(block_allowed, tile, MASKED_SCORE)

        scores = lax.map(score_tile, (head_kv, allowed, key_segment))
        row_max = jnp.max(jnp.max(scores, axis=-1), axis=0)

        def value_step(state, inputs):
            block_scores, kv_block, block_allowed, block_segment = inputs
            prob_total, weighted = state
            probs = jnp.where(block_allowed, jnp.exp(block_scores - row_max[:, None]), 0.0)
            weights = probs.astype(jnp.bfloat16)
            update = jnp.dot(weights, kv_block[:, HD:], preferred_element_type=jnp.float32)
            return ((prob_total + jnp.sum(probs, axis=-1), weighted + update), None)

        start_state = (
            jnp.zeros((row_count,), jnp.float32),
            jnp.zeros((row_count, HD), jnp.float32),
        )
        final_state, unused_rest = lax.scan(
            value_step, start_state, (scores, head_kv, allowed, key_segment)
        )
        prob_total, weighted = final_state
        return weighted / prob_total[:, None]

    per_head = lax.map(one_head, jnp.arange(head_total, dtype=jnp.int32))
    result = jnp.transpose(per_head, (1, 0, 2)).reshape(row_count, head_total * HD)
    context = jnp.where(is_live[:, None], result, 0.0).astype(jnp.bfloat16)
    live_rows = jnp.where(is_live[:, None, None], packed, jnp.zeros((), jnp.bfloat16))
    page_total = row_count // PAGE
    page_rows = (
        live_rows.reshape(page_total, PAGE, kv_heads, 2 * HD)
        .transpose(0, 2, 1, 3)
        .reshape(page_total, kv_heads, PAGE * 2 * HD)
    )
    tp_count = lax.axis_size("tp")
    slots_here = page_total // tp_count
    local_table = page_table[0]
    slot_hits = (local_table[None, :] == jnp.arange(page_total, dtype=jnp.int32)[:, None]).astype(
        jnp.int32
    )
    page_order = jnp.sum(slot_hits * jnp.arange(page_total, dtype=jnp.int32)[None, :], axis=1)
    page_order = page_order.reshape(tp_count, slots_here).T
    outgoing = page_rows[page_order].reshape(slots_here, tp_count * kv_heads, PAGE * 2 * HD)
    cache = lax.all_to_all(outgoing, "tp", split_axis=1, concat_axis=1, tiled=True)
    return (context, cache)


def solution(mesh):
    in_specs = (
        P("req", None),
        P(),
        P(None, "tp"),
        P(None, "tp"),
        P(None, "tp"),
        P(),
        P(),
        P("req", None),
    )
    out_specs = (P("req", "tp"), P(("req", "tp"), None, None))
    return jax.shard_map(
        per_device, mesh=mesh, in_specs=in_specs, out_specs=out_specs, check_vma=False
    )
```

profile of v0, /device:TPU:0, one launch (start us, length us, event | category | flops | bytes accessed | tf_op | source)
XLA Modules:
  0.0 585.2 jit_solution(6345758154150786768)
XLA Ops:
  5.3 2.2 convolution_convert_fusion
  10.7 2.2 fusion.38
  17.6 3.0 collective-permute-start.3
  20.6 4.4 collective-permute-start.2
  25.0 4.3 collective-permute-start.1
  29.3 2.0 collective-permute-start
  38.8 2.0 fusion.22
  41.5 2.0 reshape.233
  43.6 2.5 gather_fusion
  49.3 4.9 all-to-all-start
  59.4 2.9 fusion.35
  71.2 508.7 %while.61 = (s32[]{:T(128)}, bf16[8,256,80]{1,2,0:T(8,128)(2,1)}, s32[8]{0:T(128)}, bf16[5,256,2,160]{3,1,0,2:T(8,128)(2,1)}, bf16[256,8,80]{0,2,1:T(8,128)(2,1)...) while((s32[]{:T(128)}, bf16[8,256,80]{1,2,0:T(8,128)(2,1)}, ...), condition=%wide.region_15.16_spmd.clone, body=%wide.region_8.15_spmd.clone.sunk | while | flops 24178716 | bytes 5789707 | solution.py:148
  77.3 2.0 fusion.52
  79.3 2.0 dynamic-slice_bitcast_fusion.6
  81.3 14.1 %while.62 = (s32[]{:T(128)}, f32[5,256,256]{1,2,0:T(8,128)}, pred[5,256,256]{2,1,0:T(32,128)(4,1)}, bf16[5,256,160]{2,1,0:T(8,128)(2,1)}, bf16[256,80]{1,0:T(8,128)(2,1)S(1)}, /*index=5*/s32[]{:T(128)}) while((s32[]{:T(128)}, f32[5,256,256]{1,2,0:T(8,128)}, pred[5,256,256]{2,1,0:T(32,128)(4,1)}, bf16[5,256,160]{2,1,0:T(8,128)(2,1)}, ...), condition=%wide.region_10.10_spmd, body=%wide.region_9.9_spmd.sunk | while | flops 10616834 | bytes 884825 | solution.py:127
  96.8 36.5 %while.63 = (s32[]{:T(128)}, f32[256]{0:T(256)S(1)}, f32[256,80]{0,1:T(8,128)}, pred[5,256,256]{2,1,0:T(32,128)(4,1)}, f32[5,256,256]{1,2,0:T(8,128)}, /*index=5...) while((s32[]{:T(128)}, f32[256]{0:T(256)S(1)}, f32[256,80]{0,1:T(8,128)}, ...), condition=%wide.region_14.14_spmd.clone, body=%wide.region_12.13_spmd.clone.sunk | while | flops 10920195 | bytes 2103424 | solution.py:142
  115.7 1.9 convolution_add_fusion.2
  140.8 2.0 fusion.52
  142.9 2.0 dynamic-slice_bitcast_fusion.6
  144.8 14.1 %while.62 = (s32[]{:T(128)}, f32[5,256,256]{1,2,0:T(8,128)}, pred[5,256,256]{2,1,0:T(32,128)(4,1)}, bf16[5,256,160]{2,1,0:T(8,128)(2,1)}, bf16[256,80]{1,0:T(8,128)(2,1)S(1)}, /*index=5*/s32[]{:T(128)}) while((s32[]{:T(128)}, f32[5,256,256]{1,2,0:T(8,128)}, pred[5,256,256]{2,1,0:T(32,128)(4,1)}, bf16[5,256,160]{2,1,0:T(8,128)(2,1)}, ...), condition=%wide.region_10.10_spmd, body=%wide.region_9.9_spmd.sunk | while | flops 10616834 | bytes 884825 | solution.py:127
  160.4 36.5 %while.63 = (s32[]{:T(128)}, f32[256]{0:T(256)S(1)}, f32[256,80]{0,1:T(8,128)}, pred[5,256,256]{2,1,0:T(32,128)(4,1)}, f32[5,256,256]{1,2,0:T(8,128)}, /*index=5...) while((s32[]{:T(128)}, f32[256]{0:T(256)S(1)}, f32[256,80]{0,1:T(8,128)}, ...), condition=%wide.region_14.14_spmd.clone, body=%wide.region_12.13_spmd.clone.sunk | while | flops 10920195 | bytes 2103424 | solution.py:142
  186.6 1.9 convolution_add_fusion.2
  204.4 2.0 fusion.52
  206.4 2.0 dynamic-slice_bitcast_fusion.6
  208.4 14.1 %while.62 = (s32[]{:T(128)}, f32[5,256,256]{1,2,0:T(8,128)}, pred[5,256,256]{2,1,0:T(32,128)(4,1)}, bf16[5,256,160]{2,1,0:T(8,128)(2,1)}, bf16[256,80]{1,0:T(8,128)(2,1)S(1)}, /*index=5*/s32[]{:T(128)}) while((s32[]{:T(128)}, f32[5,256,256]{1,2,0:T(8,128)}, pred[5,256,256]{2,1,0:T(32,128)(4,1)}, bf16[5,256,160]{2,1,0:T(8,128)(2,1)}, ...), condition=%wide.region_10.10_spmd, body=%wide.region_9.9_spmd.sunk | while | flops 10616834 | bytes 884825 | solution.py:127
  224.0 36.5 %while.63 = (s32[]{:T(128)}, f32[256]{0:T(256)S(1)}, f32[256,80]{0,1:T(8,128)}, pred[5,256,256]{2,1,0:T(32,128)(4,1)}, f32[5,256,256]{1,2,0:T(8,128)}, /*index=5...) while((s32[]{:T(128)}, f32[256]{0:T(256)S(1)}, f32[256,80]{0,1:T(8,128)}, ...), condition=%wide.region_14.14_spmd.clone, body=%wide.region_12.13_spmd.clone.sunk | while | flops 10920195 | bytes 2103424 | solution.py:142
  235.6 1.9 convolution_add_fusion.2
  268.0 2.0 fusion.52
  270.0 2.0 dynamic-slice_bitcast_fusion.6
  272.0 14.1 %while.62 = (s32[]{:T(128)}, f32[5,256,256]{1,2,0:T(8,128)}, pred[5,256,256]{2,1,0:T(32,128)(4,1)}, bf16[5,256,160]{2,1,0:T(8,128)(2,1)}, bf16[256,80]{1,0:T(8,128)(2,1)S(1)}, /*index=5*/s32[]{:T(128)}) while((s32[]{:T(128)}, f32[5,256,256]{1,2,0:T(8,128)}, pred[5,256,256]{2,1,0:T(32,128)(4,1)}, bf16[5,256,160]{2,1,0:T(8,128)(2,1)}, ...), condition=%wide.region_10.10_spmd, body=%wide.region_9.9_spmd.sunk | while | flops 10616834 | bytes 884825 | solution.py:127
  287.6 36.5 %while.63 = (s32[]{:T(128)}, f32[256]{0:T(256)S(1)}, f32[256,80]{0,1:T(8,128)}, pred[5,256,256]{2,1,0:T(32,128)(4,1)}, f32[5,256,256]{1,2,0:T(8,128)}, /*index=5...) while((s32[]{:T(128)}, f32[256]{0:T(256)S(1)}, f32[256,80]{0,1:T(8,128)}, ...), condition=%wide.region_14.14_spmd.clone, body=%wide.region_12.13_spmd.clone.sunk | while | flops 10920195 | bytes 2103424 | solution.py:142
  313.8 1.9 convolution_add_fusion.2
  331.6 2.0 fusion.52
  333.6 2.0 dynamic-slice_bitcast_fusion.6
  335.6 14.1 %while.62 = (s32[]{:T(128)}, f32[5,256,256]{1,2,0:T(8,128)}, pred[5,256,256]{2,1,0:T(32,128)(4,1)}, bf16[5,256,160]{2,1,0:T(8,128)(2,1)}, bf16[256,80]{1,0:T(8,128)(2,1)S(1)}, /*index=5*/s32[]{:T(128)}) while((s32[]{:T(128)}, f32[5,256,256]{1,2,0:T(8,128)}, pred[5,256,256]{2,1,0:T(32,128)(4,1)}, bf16[5,256,160]{2,1,0:T(8,128)(2,1)}, ...), condition=%wide.region_10.10_spmd, body=%wide.region_9.9_spmd.sunk | while | flops 10616834 | bytes 884825 | solution.py:127
  351.2 36.5 %while.63 = (s32[]{:T(128)}, f32[256]{0:T(256)S(1)}, f32[256,80]{0,1:T(8,128)}, pred[5,256,256]{2,1,0:T(32,128)(4,1)}, f32[5,256,256]{1,2,0:T(8,128)}, /*index=5...) while((s32[]{:T(128)}, f32[256]{0:T(256)S(1)}, f32[256,80]{0,1:T(8,128)}, ...), condition=%wide.region_14.14_spmd.clone, body=%wide.region_12.13_spmd.clone.sunk | while | flops 10920195 | bytes 2103424 | solution.py:142
  395.2 2.0 fusion.52
  397.2 2.0 dynamic-slice_bitcast_fusion.6
  399.2 14.1 %while.62 = (s32[]{:T(128)}, f32[5,256,256]{1,2,0:T(8,128)}, pred[5,256,256]{2,1,0:T(32,128)(4,1)}, bf16[5,256,160]{2,1,0:T(8,128)(2,1)}, bf16[256,80]{1,0:T(8,128)(2,1)S(1)}, /*index=5*/s32[]{:T(128)}) while((s32[]{:T(128)}, f32[5,256,256]{1,2,0:T(8,128)}, pred[5,256,256]{2,1,0:T(32,128)(4,1)}, bf16[5,256,160]{2,1,0:T(8,128)(2,1)}, ...), condition=%wide.region_10.10_spmd, body=%wide.region_9.9_spmd.sunk | while | flops 10616834 | bytes 884825 | solution.py:127
  414.8 36.5 %while.63 = (s32[]{:T(128)}, f32[256]{0:T(256)S(1)}, f32[256,80]{0,1:T(8,128)}, pred[5,256,256]{2,1,0:T(32,128)(4,1)}, f32[5,256,256]{1,2,0:T(8,128)}, /*index=5...) while((s32[]{:T(128)}, f32[256]{0:T(256)S(1)}, f32[256,80]{0,1:T(8,128)}, ...), condition=%wide.region_14.14_spmd.clone, body=%wide.region_12.13_spmd.clone.sunk | while | flops 10920195 | bytes 2103424 | solution.py:142
  458.8 2.0 fusion.52
  460.8 2.0 dynamic-slice_bitcast_fusion.6
  462.8 14.1 %while.62 = (s32[]{:T(128)}, f32[5,256,256]{1,2,0:T(8,128)}, pred[5,256,256]{2,1,0:T(32,128)(4,1)}, bf16[5,256,160]{2,1,0:T(8,128)(2,1)}, bf16[256,80]{1,0:T(8,128)(2,1)S(1)}, /*index=5*/s32[]{:T(128)}) while((s32[]{:T(128)}, f32[5,256,256]{1,2,0:T(8,128)}, pred[5,256,256]{2,1,0:T(32,128)(4,1)}, bf16[5,256,160]{2,1,0:T(8,128)(2,1)}, ...), condition=%wide.region_10.10_spmd, body=%wide.region_9.9_spmd.sunk | while | flops 10616834 | bytes 884825 | solution.py:127
  478.3 36.5 %while.63 = (s32[]{:T(128)}, f32[256]{0:T(256)S(1)}, f32[256,80]{0,1:T(8,128)}, pred[5,256,256]{2,1,0:T(32,128)(4,1)}, f32[5,256,256]{1,2,0:T(8,128)}, /*index=5...) while((s32[]{:T(128)}, f32[256]{0:T(256)S(1)}, f32[256,80]{0,1:T(8,128)}, ...), condition=%wide.region_14.14_spmd.clone, body=%wide.region_12.13_spmd.clone.sunk | while | flops 10920195 | bytes 2103424 | solution.py:142
  522.4 2.0 fusion.52
  524.4 2.0 dynamic-slice_bitcast_fusion.6
  526.4 14.1 %while.62 = (s32[]{:T(128)}, f32[5,256,256]{1,2,0:T(8,128)}, pred[5,256,256]{2,1,0:T(32,128)(4,1)}, bf16[5,256,160]{2,1,0:T(8,128)(2,1)}, bf16[256,80]{1,0:T(8,128)(2,1)S(1)}, /*index=5*/s32[]{:T(128)}) while((s32[]{:T(128)}, f32[5,256,256]{1,2,0:T(8,128)}, pred[5,256,256]{2,1,0:T(32,128)(4,1)}, bf16[5,256,160]{2,1,0:T(8,128)(2,1)}, ...), condition=%wide.region_10.10_spmd, body=%wide.region_9.9_spmd.sunk | while | flops 10616834 | bytes 884825 | solution.py:127
  541.9 36.5 %while.63 = (s32[]{:T(128)}, f32[256]{0:T(256)S(1)}, f32[256,80]{0,1:T(8,128)}, pred[5,256,256]{2,1,0:T(32,128)(4,1)}, f32[5,256,256]{1,2,0:T(8,128)}, /*index=5...) while((s32[]{:T(128)}, f32[256]{0:T(256)S(1)}, f32[256,80]{0,1:T(8,128)}, ...), condition=%wide.region_14.14_spmd.clone, body=%wide.region_12.13_spmd.clone.sunk | while | flops 10920195 | bytes 2103424 | solution.py:142
  (568 shorter events, 479.5 us)
Async XLA Ops:
  0.6 58.7 %copy-start = (bf16[2560,640]{1,0:T(8,128)(2,1)S(1)}, bf16[2560,640]{1,0:T(8,128)(2,1)}, u32[]{:S(2)}) copy-start(bf16[2560,640]{1,0:T(8,128)(2,1)} %param.16) | copy-start | bytes 9830404
  0.6 3.2 copy-start.20
  0.7 3.2 copy-start.21
  0.7 4.6 copy-start.22
  3.7 7.0 %copy-start.19 = (f32[256]{0:T(256)}, f32[256]{0:T(256)S(1)}, u32[]{:S(2)}) copy-start(f32[256]{0:T(256)S(1)} %add_rsqrt_fusion) | copy-start | bytes 3076
  3.9 1.4 copy-start.15
  3.9 1.4 copy-start.17
  3.9 1.4 copy-start.18
  4.6 0.7 copy-start.13
  5.3 26.1 %copy-start.9 = (s32[256]{0:T(256)}, s32[256]{0:T(256)S(1)}, u32[]{:S(2)}) copy-start(s32[256]{0:T(256)S(1)} %get-tuple-element.318) | copy-start | bytes 3076
  7.5 0.6 copy-start.7
  9.1 3.7 copy-start.3
  9.1 3.7 copy-start.5
  17.6 51.4 %collective-permute-start.3 = (bf16[256,2,160]{2,0,1:T(8,128)(2,1)}, bf16[256,2,160]{2,0,1:T(8,128)(2,1)}, u32[]{:S(2)}, u32[]{:S(2)}) collective-permute-start(bf16[256,2,160]{2,0,1:T(8,128)(2,1)} %pad_maximum_fusion.1), channel_id=1, source_target_pairs={{0,4},{4,8},{8,12},{12,16},{16,20},{20,24},{24,28},{1,5},{5,9},{9,... | collective-permute-start | bytes 491528 | tf_op jit(solution)/shard_map/ppermute | solution.py:19
  20.6 47.4 %collective-permute-start.2 = (bf16[256,2,160]{2,0,1:T(8,128)(2,1)}, bf16[256,2,160]{2,0,1:T(8,128)(2,1)}, u32[]{:S(2)}, u32[]{:S(2)}) collective-permute-start(bf16[256,2,160]{2,0,1:T(8,128)(2,1)} %pad_maximum_fusion.1), channel_id=1, source_target_pairs={{0,8},{4,12},{8,16},{12,20},{16,24},{20,28},{1,9},{5,13},{9,17},{1... | collective-permute-start | bytes 491528 | tf_op jit(solution)/shard_map/ppermute | solution.py:19
  25.0 42.0 %collective-permute-start.1 = (bf16[256,2,160]{2,0,1:T(8,128)(2,1)}, bf16[256,2,160]{2,0,1:T(8,128)(2,1)}, u32[]{:S(2)}, u32[]{:S(2)}) collective-permute-start(bf16[256,2,160]{2,0,1:T(8,128)(2,1)} %pad_maximum_fusion.1), channel_id=1, source_target_pairs={{0,12},{4,16},{8,20},{12,24},{16,28},{1,13},{5,17},{9,21},{13,25},... | collective-permute-start | bytes 491528 | tf_op jit(solution)/shard_map/ppermute | solution.py:19
  29.3 36.7 %collective-permute-start = (bf16[256,2,160]{2,0,1:T(8,128)(2,1)}, bf16[256,2,160]{2,0,1:T(8,128)(2,1)}, u32[]{:S(2)}, u32[]{:S(2)}) collective-permute-start(bf16[256,2,160]{2,0,1:T(8,128)(2,1)} %pad_maximum_fusion.1), channel_id=1, source_target_pairs={{0,16},{4,20},{8,24},{12,28},{1,17},{5,21},{9,25},{13,29},{2,18},{... | collective-permute-start | bytes 491528 | tf_op jit(solution)/shard_map/ppermute | solution.py:19
  38.7 4.8 copy-start.11
  38.7 15.5 %copy-start.10 = (s32[256]{0:T(256)S(1)}, s32[256]{0:T(256)}, u32[]{:S(2)}) copy-start(s32[256]{0:T(256)} %copy-done.9) | copy-start | bytes 3076
  38.7 15.5 %copy-start.12 = (s32[256]{0:T(256)S(1)}, s32[256]{0:T(256)}, u32[]{:S(2)}) copy-start(s32[256]{0:T(256)} %get-tuple-element.317) | copy-start | bytes 3076
  38.8 16.0 %copy-start.16 = (s32[4,1]{0,1:T(1,128)S(1)}, s32[4,1]{0,1:T(1,128)}, u32[]{:S(2)}) copy-start(s32[4,1]{0,1:T(1,128)} %copy-done.15) | copy-start | bytes 52
  49.3 534.2 %all-to-all-start = ((bf16[4,8,2560]{2,0,1:T(4,128)(2,1)}), bf16[4,8,2560]{2,0,1:T(4,128)(2,1)}, u32[]{:S(2)}, u32[]{:S(2)}) async-start(bf16[4,8,2560]{2,0,1:T(4,128)(2,1)} %copy.105), calls=%async_computation | async-start | bytes 327680 | tf_op jit(solution)/shard_map/all_to_all | solution.py:167
  59.3 2.9 copy-start.4
  59.3 2.9 copy-start.6
  59.3 3.7 copy-start.8
  59.3 4.3 copy-start.14
  64.2 5.7 copy-start.2
  70.2 1.1 copy-start.1
where the time goes:
time: 597 us; the launch traced here: 585 us
  local copies, waits for them, and re-layouts  311 us (52%)
  matrix products  120 us (20%)
  other arithmetic  102 us (17%)
  loops' own time  32.6 us (5%)
  starting transfers between devices  18.6 us (3%)
    dynamic_slice x80, local copies, waits for them, and re-layouts, one_head(): lax.scan(value_step, start_state, (scores, head_kv, allowed, key_segment))  109 us
    squeeze x80, local copies, waits for them, and re-layouts, one_head(): scores = lax.map(score_tile, (head_kv, allowed, key_segment))  99.8 us
    dot_general x40, matrix products, value_step(): jnp.dot(weights, kv_block[:, HD:], preferred_element_type=jnp.float32)  76.5 us
    reduce_sum x40, other arithmetic, value_step(): return ((prob_total + jnp.sum(probs, axis=-1), weighted + update), None)  41.5 us
    dynamic_slice x80, local copies, waits for them, and re-layouts, one_head(): scores = lax.map(score_tile, (head_kv, allowed, key_segment))  39.4 us
    dot_general x40, matrix products, score_tile(): lax.dot_general(head_queries, kv_block[:, :HD], (((1,), (1,)), ((), ())),...  35.9 us
    another operation x1, loops' own time, per_device(): per_head = lax.map(one_head, jnp.arange(head_total, dtype=jnp.int32))  30.9 us
    and x8, other arithmetic, per_device(): allowed & (key_index[:, None, :] <= slot_index[None, :, None])  16.2 us
  transfers between devices with their start and end apart: 5, of which 0 were waited for; matrix products, arithmetic and copies ran while one was open for 88% of the time, Pallas kernels for 0%

commit v1 on v0

v1 whole, which is shorter than its diff:
```python
import functools
import math

import jax
import jax.numpy as jnp
from jax import lax
from jax.experimental import pallas as pl
from jax.experimental.pallas import tpu as pltpu
from jax.sharding import PartitionSpec as P

HD = 80
WINDOW = 4096
PAGE = 16
NORM_EPS = 1e-05
ROPE_BASE = 10000.0
MASKED = -1e30
ROW = 2 * HD
ONES = 16
MESH = pl.DeviceIdType.MESH
F32 = jnp.float32
BF16 = jnp.bfloat16


def meta(slot, counts, pads):
    first = jnp.zeros_like(slot)
    last = jnp.zeros_like(slot)
    start = jnp.int32(0)
    for i in range(counts.shape[0]):
        slots = counts[i] * PAGE
        inside = (slot >= start) & (slot < start + slots)
        first = jnp.where(inside, start, first)
        last = jnp.where(inside, start + slots - pads[i] - 1, last)
        start = start + slots
    return first, last


def rotary(u, cosine, sine):
    half = HD // 2
    u1, u2 = u[:half], u[half:]
    return jnp.concatenate([u1 * cosine - u2 * sine, u2 * cosine + u1 * sine], axis=0)


def kernel(
    n_req, n_tp, reach, phases,
    counts, pads, table, gain, tokens_hbm, wk_hbm, wv_hbm, wq_hbm,
    context_ref, cache_ref,
    tokens, wk, wv, wq, kv_own, kv_in, page_out, page_in,
    load_sem, kv_send, kv_recv, page_send, page_recv,
):
    rows = tokens.shape[0]
    kvh = wk.shape[1] // HD
    heads = wq.shape[1] // HD
    group = heads // kvh
    me = lax.axis_index("req")
    my_tp = lax.axis_index("tp")

    loads = [
        pltpu.make_async_copy(src, dst, load_sem.at[i])
        for i, (src, dst) in enumerate(
            ((tokens_hbm, tokens), (wk_hbm, wk), (wv_hbm, wv), (wq_hbm, wq))
        )
    ]
    for load in loads:
        load.start()

    barrier = pltpu.get_barrier_semaphore()
    for d in range(1, reach + 1):
        @pl.when(me + d < n_req)
        def _():
            pl.semaphore_signal(barrier, inc=1, device_id={"req": me + d}, device_id_type=MESH)

        @pl.when(me - d >= 0)
        def _():
            pl.semaphore_signal(barrier, inc=1, device_id={"req": me - d}, device_id_type=MESH)
    for o in range(1, n_tp):
        pl.semaphore_signal(
            barrier, inc=1, device_id={"tp": lax.rem(my_tp + o, n_tp)}, device_id_type=MESH
        )

    block_start = me * rows
    slot = block_start + lax.broadcasted_iota(jnp.int32, (1, rows), 1)
    first, last = meta(slot, counts, pads)
    position = (slot - first).astype(F32)
    live = slot <= last
    high = jnp.minimum(slot, last)
    index = lax.broadcasted_iota(jnp.int32, (HD // 2, 1), 0).astype(F32)
    frequency = jnp.exp(index * (-2.0 * math.log(ROPE_BASE) / HD))
    angle = frequency * position
    cosine, sine = jnp.cos(angle), jnp.sin(angle)

    loads[0].wait()
    x = tokens[...].astype(F32)
    scale = lax.rsqrt(jnp.mean(x * x, axis=-1, keepdims=True) + NORM_EPS)
    tokens[...] = (x * scale * gain[...]).astype(BF16)

    loads[1].wait()
    key = jnp.dot(tokens[...], wk[...], preferred_element_type=F32).T
    loads[2].wait()
    value = jnp.dot(tokens[...], wv[...], preferred_element_type=F32).T
    for g in range(kvh):
        at = g * HD
        kv_own[g * ROW : g * ROW + HD] = rotary(key[at : at + HD], cosine, sine).astype(BF16)
        kv_own[g * ROW + HD : (g + 1) * ROW] = value[at : at + HD].astype(BF16)

    ahead = jnp.minimum(reach, n_req - 1 - me)
    behind = jnp.minimum(reach, me)
    pl.semaphore_wait(barrier, ahead + behind + n_tp - 1)

    def kv_copy(d):
        return pltpu.make_async_remote_copy(
            src_ref=kv_own,
            dst_ref=kv_in.at[d - 1],
            send_sem=kv_send.at[d - 1],
            recv_sem=kv_recv.at[d - 1],
            device_id={"req": me + d},
            device_id_type=MESH,
        )

    for d in range(1, reach + 1):
        @pl.when(me + d < n_req)
        def _():
            kv_copy(d).start()

        @pl.when(me - d < 0)
        def _():
            kv_in[d - 1] = jnp.zeros(kv_in.shape[1:], BF16)

    slots_here = rows // PAGE // n_tp
    live_rows = slots_here * kvh
    fold = 16 // live_rows
    pieces = PAGE // fold
    span = pieces * ROW
    bits = [int(math.log2(v)) for v in (kvh, slots_here, fold, n_tp)]
    r = lax.broadcasted_iota(jnp.int32, (pieces * n_tp * 16, 1), 0)
    h_r = r & (kvh - 1)
    r = r >> bits[0]
    slot_r = r & (slots_here - 1)
    r = r >> bits[1]
    fold_r = r & (fold - 1)
    r = r >> bits[2]
    tp_r = r & (n_tp - 1)
    piece_r = r >> bits[3]
    place_r = h_r + kvh * (fold_r * pieces + piece_r + PAGE * (tp_r * slots_here + slot_r))
    in_block = lax.broadcasted_iota(jnp.int32, (1, rows), 1)
    page_at = jnp.zeros_like(in_block)
    for p in range(rows // PAGE):
        page_at = jnp.where((in_block >> 4) == p, table[0, p], page_at)
    place_t = jnp.where(live, kvh * ((in_block & (PAGE - 1)) + PAGE * page_at), -kvh)
    place_c = jnp.concatenate([place_t + h for h in range(kvh)], axis=1)
    pick = jnp.where(place_r == place_c, 1.0, 0.0).astype(BF16)
    kv_wide = jnp.concatenate([kv_own[g * ROW : (g + 1) * ROW] for g in range(kvh)], axis=1)
    placed = lax.dot_general(
        pick, kv_wide, (((1,), (1,)), ((), ())), preferred_element_type=F32
    )
    wide = jnp.concatenate(
        [placed[i * n_tp * 16 : (i + 1) * n_tp * 16] for i in range(pieces)], axis=1
    ).astype(BF16)
    for t in range(n_tp):
        page_out[t] = wide[t * 16 : (t + 1) * 16]

    def page_copy(o):
        to = lax.rem(my_tp + o, n_tp)
        return pltpu.make_async_remote_copy(
            src_ref=page_out.at[to],
            dst_ref=page_in.at[o],
            send_sem=page_send.at[o],
            recv_sem=page_recv.at[o],
            device_id={"tp": to},
            device_id_type=MESH,
        )

    for o in range(1, n_tp):
        page_copy(o).start()
    page_in[0] = page_out[my_tp]

    loads[3].wait()
    query = jnp.dot(tokens[...], wq[...], preferred_element_type=F32).T
    queries = []
    for g in range(kvh):
        parts = []
        for h in range(g * group, (g + 1) * group):
            parts.append(rotary(query[h * HD : (h + 1) * HD], cosine, sine).astype(BF16))
        queries.append(jnp.concatenate(parts, axis=1))

    factor = math.log2(math.e) / math.sqrt(HD)
    ones = jnp.ones((ONES, rows), BF16)
    state = [None] * kvh
    for blocks in phases:
        bias = []
        for d in blocks:
            if d:
                @pl.when(me - d >= 0)
                def _():
                    kv_copy(d).wait_recv()
            at = slot[:, :1] - d * rows + lax.broadcasted_iota(jnp.int32, (rows, 1), 0)
            ok = (at >= first) & (at <= high)
            if (d + 1) * rows > WINDOW:
                ok = ok & (slot - at < WINDOW)
            bias.append(jnp.where(ok, 0.0, MASKED))
        for g in range(kvh):
            scores, values = [], []
            for d, b in zip(blocks, bias):
                src = kv_own if d == 0 else kv_in.at[d - 1]
                s = lax.dot_general(
                    src[g * ROW : g * ROW + HD], queries[g], (((0,), (0,)), ((), ())),
                    preferred_element_type=F32,
                )
                scores.append(s * factor + jnp.concatenate([b] * group, axis=1))
                values.append(
                    jnp.concatenate([src[g * ROW + HD : (g + 1) * ROW], ones], axis=0)
                )
            top = functools.reduce(
                jnp.maximum, [jnp.max(s, axis=0, keepdims=True) for s in scores]
            )
            if state[g] is not None:
                top = jnp.maximum(top, state[g][0])
            total = None
            for s, v in zip(scores, values):
                w = jnp.exp2(s - top).astype(BF16)
                part = jnp.dot(v, w, preferred_element_type=F32)
                total = part if total is None else total + part
            if state[g] is not None:
                total = total + state[g][1] * jnp.exp2(state[g][0] - top)
            state[g] = (top, total)

    columns = []
    for g in range(kvh):
        acc = state[g][1]
        out = acc[:HD] / acc[HD : HD + 1]
        for j in range(group):
            columns.append(jnp.where(live, out[:, j * rows : (j + 1) * rows], 0.0))
    context_ref[...] = jnp.concatenate(columns, axis=0).T.astype(BF16)

    for o in range(1, n_tp):
        page_copy(o).wait_recv()
    source = lax.broadcasted_iota(jnp.int32, (1, n_tp * 16), 1)
    from_tp = (my_tp - (source >> 4) + n_tp) & (n_tp - 1)
    in_tile = source & 15
    fold_s = in_tile >> (bits[0] + bits[1])
    slot_s = (in_tile >> bits[0]) & (slots_here - 1)
    h_s = in_tile & (kvh - 1)
    goal_s = (slot_s * n_tp + from_tp) * kvh + h_s
    goal = lax.broadcasted_iota(jnp.int32, (slots_here * n_tp * kvh, 1), 0)
    arrived = page_in[...].reshape(n_tp * 16, span)
    lanes = []
    for f in range(fold):
        pick_f = jnp.where((goal == goal_s) & (fold_s == f), 1.0, 0.0).astype(BF16)
        lanes.append(jnp.dot(pick_f, arrived, preferred_element_type=F32))
    pages = jnp.concatenate(lanes, axis=1)
    all_heads = n_tp * kvh
    for s in range(slots_here):
        cache_ref[s] = pages[s * all_heads : (s + 1) * all_heads].astype(BF16)

    for d in range(1, reach + 1):
        @pl.when(me + d < n_req)
        def _():
            kv_copy(d).wait_send()
    for o in range(1, n_tp):
        page_copy(o).wait_send()


def per_device(tokens, norm_gain, w_query, w_key, w_value, page_counts, pad_counts, page_table):
    rows, width = tokens.shape
    n_req, n_tp = lax.axis_size("req"), lax.axis_size("tp")
    longest = min(8 * rows, rows * n_req // 2)
    reach = min(WINDOW, longest) // rows
    phases = [[0], list(range(1, reach + 1))]
    kv_rows = 2 * w_key.shape[1]
    kvh = w_key.shape[1] // HD
    slots_here = rows // PAGE // n_tp
    span = slots_here * kvh * PAGE * ROW // 16
    vmem = pl.BlockSpec(memory_space=pltpu.VMEM)
    smem = pl.BlockSpec(memory_space=pltpu.SMEM)
    hbm = pl.BlockSpec(memory_space=pltpu.HBM)
    return pl.pallas_call(
        functools.partial(kernel, n_req, n_tp, reach, phases),
        out_shape=(
            jax.ShapeDtypeStruct((rows, w_query.shape[1]), BF16),
            jax.ShapeDtypeStruct((slots_here, n_tp * kvh, PAGE * ROW), BF16),
        ),
        in_specs=[smem, smem, smem, vmem, hbm, hbm, hbm, hbm],
        out_specs=(vmem, vmem),
        scratch_shapes=[
            pltpu.VMEM((rows, width), BF16),
            pltpu.VMEM(w_key.shape, BF16),
            pltpu.VMEM(w_value.shape, BF16),
            pltpu.VMEM(w_query.shape, BF16),
            pltpu.VMEM((kv_rows, rows), BF16),
            pltpu.VMEM((reach, kv_rows, rows), BF16),
            pltpu.VMEM((n_tp, 16, span), BF16),
            pltpu.VMEM((n_tp, 16, span), BF16),
            pltpu.SemaphoreType.DMA((4,)),
            pltpu.SemaphoreType.DMA((reach,)),
            pltpu.SemaphoreType.DMA((reach,)),
            pltpu.SemaphoreType.DMA((n_tp,)),
            pltpu.SemaphoreType.DMA((n_tp,)),
        ],
        compiler_params=pltpu.CompilerParams(
            collective_id=0, has_side_effects=True, vmem_limit_bytes=56 * 1024 * 1024
        ),
    )(
        page_counts, pad_counts, page_table, norm_gain.reshape(1, width),
        tokens, w_key, w_value, w_query,
    )


def solution(mesh):
    in_specs = (
        P("req", None),
        P(),
        P(None, "tp"),
        P(None, "tp"),
        P(None, "tp"),
        P(),
        P(),
        P("req", None),
    )
    out_specs = (P("req", "tp"), P(("req", "tp"), None, None))
    return jax.shard_map(
        per_device, mesh=mesh, in_specs=in_specs, out_specs=out_specs, check_vma=False
    )
```

time: 597 us -> 31.9 us (0.05)
  the two profiles are of different devices: /device:TPU:0 before, /device:TPU:29 now
where the time goes in v1:
time: 31.9 us; the launch traced here: 31.6 us
  Pallas kernels  22.5 us (71%)
  local copies, waits for them, and re-layouts  8.45 us (26%)
  between operations  0.65 us (2%)
    pallas_call x1, Pallas kernels, per_device(): pl.pallas_call(functools.partial(kernel, n_req, n_tp, reach, phases), out...  22.5 us
    unnamed x6, local copies, waits for them, and re-layouts  7.07 us
    reshape x1, local copies, waits for them, and re-layouts, per_device(): norm_gain.reshape(1, width)  1.39 us

profile of v1, /device:TPU:29, one launch (start us, length us, event | category | flops | bytes accessed | tf_op | source)
XLA Modules:
  0.0 31.6 jit_solution(17887172397777630579)
XLA Ops:
  0.6 0.0 copy-start
  0.6 1.4 %reshape.7.gain = f32[1,2560]{1,0:T(1,128)} reshape(f32[2560]{0:T(1024)} %param.9) | data formatting | bytes 20480 | tf_op jit(solution)/shard_map/reshape | solution.py:302
  2.0 2.3 %copy.10.wk_hbm = bf16[2560,160]{1,0:T(8,128)(2,1)} copy(bf16[2560,160]{0,1:T(8,128)(2,1)} %param.11) | data formatting | bytes 1638400 | tf_op args[3]
  4.4 0.0 copy-done
  4.4 1.4 %copy.11.wv_hbm = bf16[2560,160]{1,0:T(8,128)(2,1)} copy(bf16[2560,160]{0,1:T(8,128)(2,1)S(1)} %copy-done) | data formatting | bytes 1638400 | tf_op args[4]
  5.8 22.5 %shard_map.95 = (bf16[256,640]{1,0:T(8,128)(2,1)}, bf16[4,8,2560]{2,1,0:T(8,128)(2,1)}) custom-call(s32[4]{0:T(128)} %counts.1, s32[4]{0:T(128)} %pads.1, s32[1,16]{1,0:T(1,128)} %table.1, f32[1,2560]{1,0:T(1,128)} %reshape.7.gain, bf16[256,2560]{1,0:T(8,128)(2,1)} %tokens_hbm.1, bf16[2560,160]{1,0:T(8,128)(2,1)} %copy.10.wk_hbm, ...), custom_call_target="tpu_custom_call" | custom-call | tf_op jit(solution)/shard_map/pallas_call | solution.py:275
  28.3 1.7 %copy.14 = bf16[256,640]{1,0:T(8,128)(2,1)} copy(bf16[256,640]{1,0:T(8,128)(2,1)} %get-tuple-element.4) | data formatting | bytes 655360
  30.0 1.6 %copy.15 = bf16[4,8,2560]{2,1,0:T(8,128)(2,1)} copy(bf16[4,8,2560]{2,1,0:T(8,128)(2,1)} %get-tuple-element.5) | data formatting | bytes 327680
Async XLA Ops:
  0.6 3.7 %copy-start = (bf16[2560,160]{0,1:T(8,128)(2,1)S(1)}, bf16[2560,160]{0,1:T(8,128)(2,1)}, u32[]{:S(2)}) copy-start(bf16[2560,160]{0,1:T(8,128)(2,1)} %param.12) | copy-start | bytes 2457604

commit v2 on v1

--- a/solution.py
+++ b/solution.py
@@ -41,30 +41,41 @@
 
 
 def kernel(
-    n_req, n_tp, reach, phases,
+    n_req, n_tp, reach,
     counts, pads, table, gain, tokens_hbm, wk_hbm, wv_hbm, wq_hbm,
-    context_ref, cache_ref,
-    tokens, wk, wv, wq, kv_own, kv_in, page_out, page_in,
-    load_sem, kv_send, kv_recv, page_send, page_recv,
+    context_ref, pages_ref,
+    tokens, wkv, wq, kv_own, kv_in, page_out, page_in,
+    load_sem, kv_send, kv_recv, hand_send, page_send, page_recv,
 ):
     rows = tokens.shape[0]
-    kvh = wk.shape[1] // HD
+    kvh = wkv.shape[0] // ROW
     heads = wq.shape[1] // HD
     group = heads // kvh
     me = lax.axis_index("req")
     my_tp = lax.axis_index("tp")
 
+    odd = lax.rem(me, 2)
+    partner = me + 1 - 2 * odd
+    evens = range(2, reach + 1, 2)
+
+    kv_width = kvh * HD
     loads = [
         pltpu.make_async_copy(src, dst, load_sem.at[i])
         for i, (src, dst) in enumerate(
-            ((tokens_hbm, tokens), (wk_hbm, wk), (wv_hbm, wv), (wq_hbm, wq))
+            (
+                (tokens_hbm, tokens),
+                (wk_hbm, wkv.at[:kv_width]),
+                (wv_hbm, wkv.at[kv_width:]),
+                (wq_hbm, wq),
+            )
         )
     ]
     for load in loads:
         load.start()
 
     barrier = pltpu.get_barrier_semaphore()
-    for d in range(1, reach + 1):
+    pl.semaphore_signal(barrier, inc=1, device_id={"req": partner}, device_id_type=MESH)
+    for d in evens:
         @pl.when(me + d < n_req)
         def _():
             pl.semaphore_signal(barrier, inc=1, device_id={"req": me + d}, device_id_type=MESH)
@@ -91,36 +102,65 @@
     loads[0].wait()
     x = tokens[...].astype(F32)
     scale = lax.rsqrt(jnp.mean(x * x, axis=-1, keepdims=True) + NORM_EPS)
-    tokens[...] = (x * scale * gain[...]).astype(BF16)
+    tokens[...] = (x * scale * gain[...].reshape(1, -1)).astype(BF16)
 
     loads[1].wait()
-    key = jnp.dot(tokens[...], wk[...], preferred_element_type=F32).T
     loads[2].wait()
-    value = jnp.dot(tokens[...], wv[...], preferred_element_type=F32).T
+    both = lax.dot_general(
+        wkv[...], tokens[...], (((1,), (1,)), ((), ())), preferred_element_type=F32
+    )
+    key, value = both[:kv_width], both[kv_width:]
     for g in range(kvh):
         at = g * HD
         kv_own[g * ROW : g * ROW + HD] = rotary(key[at : at + HD], cosine, sine).astype(BF16)
         kv_own[g * ROW + HD : (g + 1) * ROW] = value[at : at + HD].astype(BF16)
 
-    ahead = jnp.minimum(reach, n_req - 1 - me)
-    behind = jnp.minimum(reach, me)
-    pl.semaphore_wait(barrier, ahead + behind + n_tp - 1)
-
-    def kv_copy(d):
+    ahead = jnp.minimum(reach, n_req - 1 - me) >> 1
+    behind = jnp.minimum(reach, me) >> 1
+    pl.semaphore_wait(barrier, ahead + behind + n_tp)
+
+    def head(ref, g):
+        return ref.at[g * ROW : (g + 1) * ROW]
+
+    def kv_copy(d, g):
         return pltpu.make_async_remote_copy(
-            src_ref=kv_own,
-            dst_ref=kv_in.at[d - 1],
-            send_sem=kv_send.at[d - 1],
-            recv_sem=kv_recv.at[d - 1],
+            src_ref=head(kv_own, g),
+            dst_ref=kv_in.at[d - 1, g * ROW : (g + 1) * ROW],
+            send_sem=kv_send.at[d - 1, g],
+            recv_sem=kv_recv.at[d - 1, g],
             device_id={"req": me + d},
             device_id_type=MESH,
         )
 
+    def hand_on(e, g):
+        to = e - 2 * odd
+        return pltpu.make_async_remote_copy(
+            src_ref=kv_in.at[e - 1, g * ROW : (g + 1) * ROW] if e else head(kv_own, g),
+            dst_ref=kv_in.at[to, g * ROW : (g + 1) * ROW],
+            send_sem=hand_send.at[e, g],
+            recv_sem=kv_recv.at[to, g],
+            device_id={"req": partner},
+            device_id_type=MESH,
+        )
+
+    def hands_on(e):
+        if e == 0:
+            return odd == 0
+        if e == reach:
+            return (odd == 1) & (me - e >= 0)
+        return me - e >= 0
+
+    for g in range(kvh):
+        for d in evens:
+            @pl.when(me + d < n_req)
+            def _():
+                kv_copy(d, g).start()
+
+        @pl.when(hands_on(0))
+        def _():
+            hand_on(0, g).start()
+
     for d in range(1, reach + 1):
-        @pl.when(me + d < n_req)
-        def _():
-            kv_copy(d).start()
-
         @pl.when(me - d < 0)
         def _():
             kv_in[d - 1] = jnp.zeros(kv_in.shape[1:], BF16)
@@ -185,54 +225,91 @@
     factor = math.log2(math.e) / math.sqrt(HD)
     ones = jnp.ones((ONES, rows), BF16)
     state = [None] * kvh
-    for blocks in phases:
-        bias = []
-        for d in blocks:
-            if d:
-                @pl.when(me - d >= 0)
-                def _():
-                    kv_copy(d).wait_recv()
-            at = slot[:, :1] - d * rows + lax.broadcasted_iota(jnp.int32, (rows, 1), 0)
-            ok = (at >= first) & (at <= high)
-            if (d + 1) * rows > WINDOW:
-                ok = ok & (slot - at < WINDOW)
-            bias.append(jnp.where(ok, 0.0, MASKED))
-        for g in range(kvh):
-            scores, values = [], []
-            for d, b in zip(blocks, bias):
-                src = kv_own if d == 0 else kv_in.at[d - 1]
-                s = lax.dot_general(
-                    src[g * ROW : g * ROW + HD], queries[g], (((0,), (0,)), ((), ())),
-                    preferred_element_type=F32,
-                )
-                scores.append(s * factor + jnp.concatenate([b] * group, axis=1))
-                values.append(
-                    jnp.concatenate([src[g * ROW + HD : (g + 1) * ROW], ones], axis=0)
-                )
-            top = functools.reduce(
-                jnp.maximum, [jnp.max(s, axis=0, keepdims=True) for s in scores]
+
+    def bias_of(d):
+        at = block_start - d * rows + lax.broadcasted_iota(jnp.int32, (rows, 1), 0)
+        ok = (at >= first) & (at <= high)
+        if (d + 1) * rows > WINDOW:
+            ok = ok & (slot - at < WINDOW)
+        return jnp.where(ok, 0.0, MASKED)
+
+    def attend(g, blocks, biases):
+        scores, values = [], []
+        for d, b in zip(blocks, biases):
+            src = kv_own if d == 0 else kv_in.at[d - 1]
+            s = lax.dot_general(
+                src[g * ROW : g * ROW + HD], queries[g], (((0,), (0,)), ((), ())),
+                preferred_element_type=F32,
             )
-            if state[g] is not None:
-                top = jnp.maximum(top, state[g][0])
-            total = None
-            for s, v in zip(scores, values):
-                w = jnp.exp2(s - top).astype(BF16)
-                part = jnp.dot(v, w, preferred_element_type=F32)
-                total = part if total is None else total + part
-            if state[g] is not None:
-                total = total + state[g][1] * jnp.exp2(state[g][0] - top)
-            state[g] = (top, total)
-
-    columns = []
-    for g in range(kvh):
+            scores.append(s * factor + jnp.concatenate([b] * group, axis=1))
+            values.append(jnp.concatenate([src[g * ROW + HD : (g + 1) * ROW], ones], axis=0))
+        top = functools.reduce(
+            jnp.maximum, [jnp.max(s, axis=0, keepdims=True) for s in scores]
+        )
+        if state[g] is not None:
+            top = jnp.maximum(top, state[g][0])
+        total = None
+        for s, v in zip(scores, values):
+            w = jnp.exp2(s - top).astype(BF16)
+            part = jnp.dot(v, w, preferred_element_type=F32)
+            total = part if total is None else total + part
+        if state[g] is not None:
+            total = total + state[g][1] * jnp.exp2(state[g][0] - top)
+        state[g] = (top, total)
+
+    own_bias = [bias_of(0)]
+    for g in range(kvh):
+        attend(g, [0], own_bias)
+        for d in evens:
+            @pl.when(me - d >= 0)
+            def _():
+                kv_copy(d, g).wait_recv()
+
+            @pl.when(hands_on(d))
+            def _():
+                hand_on(d, g).start()
+    biases = [bias_of(d) for d in evens]
+    for g in range(kvh):
+        attend(g, list(evens), biases)
+    odds = range(1, reach + 1, 2)
+    biases = [bias_of(d) for d in odds]
+    for g in range(kvh):
+        for d in odds:
+            @pl.when(me - d >= 0)
+            def _():
+                kv_copy(d, g).wait_recv()
+        attend(g, list(odds), biases)
         acc = state[g][1]
         out = acc[:HD] / acc[HD : HD + 1]
         for j in range(group):
-            columns.append(jnp.where(live, out[:, j * rows : (j + 1) * rows], 0.0))
-    context_ref[...] = jnp.concatenate(columns, axis=0).T.astype(BF16)
+            at = (g * group + j) * HD
+            context_ref[at : at + HD] = jnp.where(
+                live, out[:, j * rows : (j + 1) * rows], 0.0
+            ).astype(BF16)
 
     for o in range(1, n_tp):
         page_copy(o).wait_recv()
+    pages_ref[...] = page_in[...]
+
+    for g in range(kvh):
+        for d in evens:
+            @pl.when(me + d < n_req)
+            def _():
+                kv_copy(d, g).wait_send()
+        for e in range(0, reach + 1, 2):
+            @pl.when(hands_on(e))
+            def _():
+                hand_on(e, g).wait_send()
+    for o in range(1, n_tp):
+        page_copy(o).wait_send()
+
+
+def finish(n_tp, kvh, context_t, page_in, context_ref, cache_ref):
+    context_ref[...] = context_t[...].T
+    slots_here = cache_ref.shape[0]
+    fold = 16 // (slots_here * kvh)
+    bits = [int(math.log2(v)) for v in (kvh, slots_here)]
+    my_tp = lax.axis_index("tp")
     source = lax.broadcasted_iota(jnp.int32, (1, n_tp * 16), 1)
     from_tp = (my_tp - (source >> 4) + n_tp) & (n_tp - 1)
     in_tile = source & 15
@@ -241,7 +318,7 @@
     h_s = in_tile & (kvh - 1)
     goal_s = (slot_s * n_tp + from_tp) * kvh + h_s
     goal = lax.broadcasted_iota(jnp.int32, (slots_here * n_tp * kvh, 1), 0)
-    arrived = page_in[...].reshape(n_tp * 16, span)
+    arrived = page_in[...].reshape(n_tp * 16, page_in.shape[2])
     lanes = []
     for f in range(fold):
         pick_f = jnp.where((goal == goal_s) & (fold_s == f), 1.0, 0.0).astype(BF16)
@@ -251,20 +328,13 @@
     for s in range(slots_here):
         cache_ref[s] = pages[s * all_heads : (s + 1) * all_heads].astype(BF16)
 
-    for d in range(1, reach + 1):
-        @pl.when(me + d < n_req)
-        def _():
-            kv_copy(d).wait_send()
-    for o in range(1, n_tp):
-        page_copy(o).wait_send()
-
 
 def per_device(tokens, norm_gain, w_query, w_key, w_value, page_counts, pad_counts, page_table):
     rows, width = tokens.shape
     n_req, n_tp = lax.axis_size("req"), lax.axis_size("tp")
     longest = min(8 * rows, rows * n_req // 2)
     reach = min(WINDOW, longest) // rows
-    phases = [[0], list(range(1, reach + 1))]
+    assert reach % 2 == 0 and n_req % 2 == 0
     kv_rows = 2 * w_key.shape[1]
     kvh = w_key.shape[1] // HD
     slots_here = rows // PAGE // n_tp
@@ -272,26 +342,26 @@
     vmem = pl.BlockSpec(memory_space=pltpu.VMEM)
     smem = pl.BlockSpec(memory_space=pltpu.SMEM)
     hbm = pl.BlockSpec(memory_space=pltpu.HBM)
-    return pl.pallas_call(
-        functools.partial(kernel, n_req, n_tp, reach, phases),
+    context_t, pages = pl.pallas_call(
+        functools.partial(kernel, n_req, n_tp, reach),
         out_shape=(
-            jax.ShapeDtypeStruct((rows, w_query.shape[1]), BF16),
-            jax.ShapeDtypeStruct((slots_here, n_tp * kvh, PAGE * ROW), BF16),
+            jax.ShapeDtypeStruct((w_query.shape[1], rows), BF16),
+            jax.ShapeDtypeStruct((n_tp, 16, span), BF16),
         ),
         in_specs=[smem, smem, smem, vmem, hbm, hbm, hbm, hbm],
         out_specs=(vmem, vmem),
         scratch_shapes=[
             pltpu.VMEM((rows, width), BF16),
-            pltpu.VMEM(w_key.shape, BF16),
-            pltpu.VMEM(w_value.shape, BF16),
+            pltpu.VMEM((kv_rows, width), BF16),
             pltpu.VMEM(w_query.shape, BF16),
             pltpu.VMEM((kv_rows, rows), BF16),
             pltpu.VMEM((reach, kv_rows, rows), BF16),
             pltpu.VMEM((n_tp, 16, span), BF16),
             pltpu.VMEM((n_tp, 16, span), BF16),
             pltpu.SemaphoreType.DMA((4,)),
-            pltpu.SemaphoreType.DMA((reach,)),
-            pltpu.SemaphoreType.DMA((reach,)),
+            pltpu.SemaphoreType.DMA((reach, kvh)),
+            pltpu.SemaphoreType.DMA((reach, kvh)),
+            pltpu.SemaphoreType.DMA((reach + 1, kvh)),
             pltpu.SemaphoreType.DMA((n_tp,)),
             pltpu.SemaphoreType.DMA((n_tp,)),
         ],
@@ -299,9 +369,19 @@
             collective_id=0, has_side_effects=True, vmem_limit_bytes=56 * 1024 * 1024
         ),
     )(
-        page_counts, pad_counts, page_table, norm_gain.reshape(1, width),
-        tokens, w_key, w_value, w_query,
+        page_counts, pad_counts, page_table, norm_gain,
+        tokens, w_key.T, w_value.T, w_query,
     )
+    return pl.pallas_call(
+        functools.partial(finish, n_tp, kvh),
+        out_shape=(
+            jax.ShapeDtypeStruct((rows, w_query.shape[1]), BF16),
+            jax.ShapeDtypeStruct((slots_here, n_tp * kvh, PAGE * ROW), BF16),
+        ),
+        in_specs=[vmem, vmem],
+        out_specs=(vmem, vmem),
+        compiler_params=pltpu.CompilerParams(vmem_limit_bytes=32 * 1024 * 1024),
+    )(context_t, pages)
 
 
 def solution(mesh):

time: 31.9 us -> 21 us (0.66)
  the two profiles are of different devices: /device:TPU:29 before, /device:TPU:4 now
where the time goes in v2:
time: 21 us; the launch traced here: 20.8 us
  Pallas kernels  18.3 us (87%)
  local copies, waits for them, and re-layouts  1.88 us (9%)
  between operations  0.65 us (3%)
    pallas_call x1, Pallas kernels, per_device(): pl.pallas_call(functools.partial(kernel, n_req, n_tp, reach), out_shape=(...  17.3 us
    unnamed x4, local copies, waits for them, and re-layouts  1.88 us
    pallas_call x1, Pallas kernels, per_device(): pl.pallas_call(functools.partial(finish, n_tp, kvh), out_shape=(jax.Shape...  0.95 us

profile of v2, /device:TPU:4, one launch (start us, length us, event | category | flops | bytes accessed | tf_op | source)
XLA Modules:
  0.0 20.8 jit_solution(18352025084384394365)
XLA Ops:
  0.6 17.3 %shard_map.95 = (bf16[640,256]{1,0:T(8,128)(2,1)}, bf16[4,16,1280]{2,1,0:T(8,128)(2,1)}) custom-call(s32[4]{0:T(128)} %counts.1, s32[4]{0:T(128)} %pads.1, s32[1,16]{1,0:T(1,128)} %table.1, f32[2560]{0:T(1024)} %gain.1, bf16[256,2560]{1,0:T(8,128)(2,1)} %tokens_hbm.1, bf16[160,2560]{1,0:T(8,128)(2,1)} %bitcast.2, bf16[160,2560]{1,0:T(8,128)(2,1)} %bitcast.3, ...), custom_call_target="tpu_custom_call" | custom-call | tf_op jit(solution)/shard_map/pallas_call | solution.py:345
  17.9 0.0 copy-start
  18.0 1.0 %copy-done = bf16[640,256]{1,0:T(8,128)(2,1)S(1)} copy-done((bf16[640,256]{1,0:T(8,128)(2,1)S(1)}, bf16[640,256]{1,0:T(8,128)(2,1)}, u32[]{:S(2)}) %copy-start) | copy-done | bytes 327704
  18.9 0.0 copy-start.1
  18.9 0.9 %copy-done.1 = bf16[4,16,1280]{2,1,0:T(8,128)(2,1)S(1)} copy-done((bf16[4,16,1280]{2,1,0:T(8,128)(2,1)S(1)}, bf16[4,16,1280]{2,1,0:T(8,128)(2,1)}, u32[]{:S(2)}) %copy-start.1) | copy-done | bytes 163864
  19.8 1.0 %shard_map.96 = (bf16[256,640]{1,0:T(8,128)(2,1)}, bf16[4,8,2560]{2,1,0:T(8,128)(2,1)}) custom-call(bf16[640,256]{1,0:T(8,128)(2,1)S(1)} %copy-done, bf16[4,16,1280]{2,1,0:T(8,128)(2,1)S(1)} %copy-done.1), custom_call_target="tpu_custom_call" | custom-call | tf_op jit(solution)/shard_map/pallas_call | solution.py:375
Async XLA Ops:
  17.9 1.0 %copy-start = (bf16[640,256]{1,0:T(8,128)(2,1)S(1)}, bf16[640,256]{1,0:T(8,128)(2,1)}, u32[]{:S(2)}) copy-start(bf16[640,256]{1,0:T(8,128)(2,1)} %get-tuple-element.4.context_t) | copy-start | bytes 983044
  18.9 0.9 %copy-start.1 = (bf16[4,16,1280]{2,1,0:T(8,128)(2,1)S(1)}, bf16[4,16,1280]{2,1,0:T(8,128)(2,1)}, u32[]{:S(2)}) copy-start(bf16[4,16,1280]{2,1,0:T(8,128)(2,1)} %get-tuple-element.5.page_in) | copy-start | bytes 491524

commit v3 on v2

--- a/solution.py
+++ b/solution.py
@@ -45,7 +45,7 @@
     counts, pads, table, gain, tokens_hbm, wk_hbm, wv_hbm, wq_hbm,
     context_ref, pages_ref,
     tokens, wkv, wq, kv_own, kv_in, page_out, page_in,
-    load_sem, kv_send, kv_recv, hand_send, page_send, page_recv,
+    load_sem, kv_send, kv_recv, hand_send, back_send, page_send, page_recv,
 ):
     rows = tokens.shape[0]
     kvh = wkv.shape[0] // ROW
@@ -150,9 +150,27 @@
             return (odd == 1) & (me - e >= 0)
         return me - e >= 0
 
+    square = n_req == 8 and reach == 4
+
+    def sends(d, g):
+        go = me + d < n_req
+        if square and d == 2 and g == 0:
+            go = go & ((me < 2) | (me > 3))
+        return go
+
+    def pass_back(g):
+        return pltpu.make_async_remote_copy(
+            src_ref=kv_in.at[3, g * ROW : (g + 1) * ROW],
+            dst_ref=kv_in.at[1, g * ROW : (g + 1) * ROW],
+            send_sem=back_send.at[g],
+            recv_sem=kv_recv.at[1, g],
+            device_id={"req": me - 2},
+            device_id_type=MESH,
+        )
+
     for g in range(kvh):
         for d in evens:
-            @pl.when(me + d < n_req)
+            @pl.when(sends(d, g))
             def _():
                 kv_copy(d, g).start()
 
@@ -258,10 +276,20 @@
         state[g] = (top, total)
 
     own_bias = [bias_of(0)]
+    if square:
+        @pl.when(me > 5)
+        def _():
+            kv_copy(4, 0).wait_recv()
+            pass_back(0).start()
     for g in range(kvh):
         attend(g, [0], own_bias)
+    for g in reversed(range(kvh)):
         for d in evens:
-            @pl.when(me - d >= 0)
+            due = me - d >= 0
+            if square and d == 4 and g == 0:
+                due = due & (me < 6)
+
+            @pl.when(due)
             def _():
                 kv_copy(d, g).wait_recv()
 
@@ -293,18 +321,29 @@
 
     for g in range(kvh):
         for d in evens:
-            @pl.when(me + d < n_req)
+            @pl.when(sends(d, g))
             def _():
                 kv_copy(d, g).wait_send()
         for e in range(0, reach + 1, 2):
             @pl.when(hands_on(e))
             def _():
                 hand_on(e, g).wait_send()
+    if square:
+        @pl.when(me > 5)
+        def _():
+            pass_back(0).wait_send()
     for o in range(1, n_tp):
         page_copy(o).wait_send()
 
 
-def finish(n_tp, kvh, context_t, page_in, context_ref, cache_ref):
+def finish(n_tp, kvh, context_hbm, page_hbm, context_ref, cache_ref, context_t, page_in, load_sem):
+    loads = [
+        pltpu.make_async_copy(context_hbm, context_t, load_sem.at[0]),
+        pltpu.make_async_copy(page_hbm, page_in, load_sem.at[1]),
+    ]
+    for load in loads:
+        load.start()
+    loads[0].wait()
     context_ref[...] = context_t[...].T
     slots_here = cache_ref.shape[0]
     fold = 16 // (slots_here * kvh)
@@ -318,6 +357,7 @@
     h_s = in_tile & (kvh - 1)
     goal_s = (slot_s * n_tp + from_tp) * kvh + h_s
     goal = lax.broadcasted_iota(jnp.int32, (slots_here * n_tp * kvh, 1), 0)
+    loads[1].wait()
     arrived = page_in[...].reshape(n_tp * 16, page_in.shape[2])
     lanes = []
     for f in range(fold):
@@ -362,6 +402,7 @@
             pltpu.SemaphoreType.DMA((reach, kvh)),
             pltpu.SemaphoreType.DMA((reach, kvh)),
             pltpu.SemaphoreType.DMA((reach + 1, kvh)),
+            pltpu.SemaphoreType.DMA((kvh,)),
             pltpu.SemaphoreType.DMA((n_tp,)),
             pltpu.SemaphoreType.DMA((n_tp,)),
         ],
@@ -378,9 +419,14 @@
             jax.ShapeDtypeStruct((rows, w_query.shape[1]), BF16),
             jax.ShapeDtypeStruct((slots_here, n_tp * kvh, PAGE * ROW), BF16),
         ),
-        in_specs=[vmem, vmem],
+        in_specs=[hbm, hbm],
         out_specs=(vmem, vmem),
-        compiler_params=pltpu.CompilerParams(vmem_limit_bytes=32 * 1024 * 1024),
+        scratch_shapes=[
+            pltpu.VMEM((w_query.shape[1], rows), BF16),
+            pltpu.VMEM((n_tp, 16, span), BF16),
+            pltpu.SemaphoreType.DMA((2,)),
+        ],
+        compiler_params=pltpu.CompilerParams(vmem_limit_bytes=56 * 1024 * 1024),
     )(context_t, pages)
 
 

time: 21 us -> 19.7 us (0.938)
  local copies, waits for them, and re-layouts: 1.88 us -> 0 us
  Pallas kernels: 18.3 us -> 18.8 us
    unnamed x4 -> x0, local copies, waits for them, and re-layouts: 1.88 us -> none
    pallas_call x1, Pallas kernels: 0.95 us -> 1.98 us  [per_device(): pl.pallas_call(functools.partial(finish, n_tp, kvh), out_shape=(jax.Shape...]
    pallas_call x1, Pallas kernels: 17.3 us -> 16.9 us  [per_device(): pl.pallas_call(functools.partial(kernel, n_req, n_tp, reach), out_shape=(...]
where the time goes in v3:
time: 19.7 us; the launch traced here: 19.5 us
  Pallas kernels  18.8 us (95%)
  between operations  0.64 us (3%)
    pallas_call x1, Pallas kernels, per_device(): pl.pallas_call(functools.partial(kernel, n_req, n_tp, reach), out_shape=(...  16.9 us
    pallas_call x1, Pallas kernels, per_device(): pl.pallas_call(functools.partial(finish, n_tp, kvh), out_shape=(jax.Shape...  1.98 us

profile of v3, /device:TPU:4, one launch (start us, length us, event | category | flops | bytes accessed | tf_op | source)
XLA Modules:
  0.0 19.5 jit_solution(5179100015391008847)
XLA Ops:
  0.6 16.9 %shard_map.95 = (bf16[640,256]{1,0:T(8,128)(2,1)}, bf16[4,16,1280]{2,1,0:T(8,128)(2,1)}) custom-call(s32[4]{0:T(128)} %counts.1, s32[4]{0:T(128)} %pads.1, s32[1,16]{1,0:T(1,128)} %table.1, f32[2560]{0:T(1024)} %gain.1, bf16[256,2560]{1,0:T(8,128)(2,1)} %tokens_hbm.1, bf16[160,2560]{1,0:T(8,128)(2,1)} %bitcast.2, bf16[160,2560]{1,0:T(8,128)(2,1)} %bitcast.3, ...), custom_call_target="tpu_custom_call" | custom-call | tf_op jit(solution)/shard_map/pallas_call | solution.py:385
  17.5 2.0 %shard_map.96 = (bf16[256,640]{1,0:T(8,128)(2,1)}, bf16[4,8,2560]{2,1,0:T(8,128)(2,1)}) custom-call(bf16[640,256]{1,0:T(8,128)(2,1)} %get-tuple-element.4.context_hbm, bf16[4,16,1280]{2,1,0:T(8,128)(2,1)} %get-tuple-element.5.page_hbm), custom_call_target="tpu_custom_call" | custom-call | tf_op jit(solution)/shard_map/pallas_call | solution.py:416

commit v4 on v3

--- a/solution.py
+++ b/solution.py
@@ -152,9 +152,9 @@
 
     square = n_req == 8 and reach == 4
 
-    def sends(d, g):
+    def sends(d):
         go = me + d < n_req
-        if square and d == 2 and g == 0:
+        if square and d == 2:
             go = go & ((me < 2) | (me > 3))
         return go
 
@@ -170,7 +170,7 @@
 
     for g in range(kvh):
         for d in evens:
-            @pl.when(sends(d, g))
+            @pl.when(sends(d))
             def _():
                 kv_copy(d, g).start()
 
@@ -276,17 +276,17 @@
         state[g] = (top, total)
 
     own_bias = [bias_of(0)]
-    if square:
-        @pl.when(me > 5)
-        def _():
-            kv_copy(4, 0).wait_recv()
-            pass_back(0).start()
-    for g in range(kvh):
+    for g in range(kvh):
+        if square:
+            @pl.when(me > 5)
+            def _():
+                kv_copy(4, g).wait_recv()
+                pass_back(g).start()
         attend(g, [0], own_bias)
-    for g in reversed(range(kvh)):
+    for g in range(kvh):
         for d in evens:
             due = me - d >= 0
-            if square and d == 4 and g == 0:
+            if square and d == 4:
                 due = due & (me < 6)
 
             @pl.when(due)
@@ -321,17 +321,17 @@
 
     for g in range(kvh):
         for d in evens:
-            @pl.when(sends(d, g))
+            @pl.when(sends(d))
             def _():
                 kv_copy(d, g).wait_send()
         for e in range(0, reach + 1, 2):
             @pl.when(hands_on(e))
             def _():
                 hand_on(e, g).wait_send()
-    if square:
-        @pl.when(me > 5)
-        def _():
-            pass_back(0).wait_send()
+        if square:
+            @pl.when(me > 5)
+            def _():
+                pass_back(g).wait_send()
     for o in range(1, n_tp):
         page_copy(o).wait_send()
 

time: 19.7 us -> 20.6 us (1.046)
  Pallas kernels: 18.8 us -> 19.7 us
    pallas_call x1, Pallas kernels: 16.9 us -> 17.8 us  [per_device(): pl.pallas_call(functools.partial(kernel, n_req, n_tp, reach), out_shape=(...]
where the time goes in v4:
time: 20.6 us; the launch traced here: 20.4 us
  Pallas kernels  19.7 us (96%)
  between operations  0.64 us (3%)
    pallas_call x1, Pallas kernels, per_device(): pl.pallas_call(functools.partial(kernel, n_req, n_tp, reach), out_shape=(...  17.8 us
    pallas_call x1, Pallas kernels, per_device(): pl.pallas_call(functools.partial(finish, n_tp, kvh), out_shape=(jax.Shape...  1.98 us

profile of v4, /device:TPU:4, one launch (start us, length us, event | category | flops | bytes accessed | tf_op | source)
XLA Modules:
  0.0 20.4 jit_solution(3792870949140035703)
XLA Ops:
  0.6 17.8 %shard_map.95 = (bf16[640,256]{1,0:T(8,128)(2,1)}, bf16[4,16,1280]{2,1,0:T(8,128)(2,1)}) custom-call(s32[4]{0:T(128)} %counts.1, s32[4]{0:T(128)} %pads.1, s32[1,16]{1,0:T(1,128)} %table.1, f32[2560]{0:T(1024)} %gain.1, bf16[256,2560]{1,0:T(8,128)(2,1)} %tokens_hbm.1, bf16[160,2560]{1,0:T(8,128)(2,1)} %bitcast.2, bf16[160,2560]{1,0:T(8,128)(2,1)} %bitcast.3, ...), custom_call_target="tpu_custom_call" | custom-call | tf_op jit(solution)/shard_map/pallas_call | solution.py:385
  18.4 2.0 %shard_map.96 = (bf16[256,640]{1,0:T(8,128)(2,1)}, bf16[4,8,2560]{2,1,0:T(8,128)(2,1)}) custom-call(bf16[640,256]{1,0:T(8,128)(2,1)} %get-tuple-element.4.context_hbm, bf16[4,16,1280]{2,1,0:T(8,128)(2,1)} %get-tuple-element.5.page_hbm), custom_call_target="tpu_custom_call" | custom-call | tf_op jit(solution)/shard_map/pallas_call | solution.py:416

commit v5 on v3

--- a/solution.py
+++ b/solution.py
@@ -283,8 +283,8 @@
             pass_back(0).start()
     for g in range(kvh):
         attend(g, [0], own_bias)
-    for g in reversed(range(kvh)):
-        for d in evens:
+    for d in reversed(evens):
+        for g in reversed(range(kvh)):
             due = me - d >= 0
             if square and d == 4 and g == 0:
                 due = due & (me < 6)
@@ -296,9 +296,9 @@
             @pl.when(hands_on(d))
             def _():
                 hand_on(d, g).start()
-    biases = [bias_of(d) for d in evens]
-    for g in range(kvh):
-        attend(g, list(evens), biases)
+        biases = [bias_of(d)]
+        for g in range(kvh):
+            attend(g, [d], biases)
     odds = range(1, reach + 1, 2)
     biases = [bias_of(d) for d in odds]
     for g in range(kvh):

time: 19.7 us -> 19.3 us (0.980)
  the two profiles are of different devices: /device:TPU:4 before, /device:TPU:5 now
where the time goes in v5:
time: 19.3 us; the launch traced here: 19.1 us
  Pallas kernels  18.4 us (95%)
  between operations  0.64 us (3%)
    pallas_call x1, Pallas kernels, per_device(): pl.pallas_call(functools.partial(kernel, n_req, n_tp, reach), out_shape=(...  16.5 us
    pallas_call x1, Pallas kernels, per_device(): pl.pallas_call(functools.partial(finish, n_tp, kvh), out_shape=(jax.Shape...  1.98 us

profile of v5, /device:TPU:5, one launch (start us, length us, event | category | flops | bytes accessed | tf_op | source)
XLA Modules:
  0.0 19.1 jit_solution(9255707643948720725)
XLA Ops:
  0.6 16.5 %shard_map.95 = (bf16[640,256]{1,0:T(8,128)(2,1)}, bf16[4,16,1280]{2,1,0:T(8,128)(2,1)}) custom-call(s32[4]{0:T(128)} %counts.1, s32[4]{0:T(128)} %pads.1, s32[1,16]{1,0:T(1,128)} %table.1, f32[2560]{0:T(1024)} %gain.1, bf16[256,2560]{1,0:T(8,128)(2,1)} %tokens_hbm.1, bf16[160,2560]{1,0:T(8,128)(2,1)} %bitcast.2, bf16[160,2560]{1,0:T(8,128)(2,1)} %bitcast.3, ...), custom_call_target="tpu_custom_call" | custom-call | tf_op jit(solution)/shard_map/pallas_call | solution.py:385
  17.1 2.0 %shard_map.96 = (bf16[256,640]{1,0:T(8,128)(2,1)}, bf16[4,8,2560]{2,1,0:T(8,128)(2,1)}) custom-call(bf16[640,256]{1,0:T(8,128)(2,1)} %get-tuple-element.4.context_hbm, bf16[4,16,1280]{2,1,0:T(8,128)(2,1)} %get-tuple-element.5.page_hbm), custom_call_target="tpu_custom_call" | custom-call | tf_op jit(solution)/shard_map/pallas_call | solution.py:416
